TPU v7x, 128 devices: a whole 4x4x4 slice. The times are simulated.
128 devices in a mesh: row: 16 (over y_hi, z, core), feat: 8 (over y_lo, x).
Axes of the slice: x: 4, y: 4 (y_hi: 2, y_lo: 2; y = y_hi * 2 + y_lo), z: 4, core: 2. Of those that a mesh axis runs over, the one named last changes fastest.
Arguments:
- queries: float32 [2, 768, 16384], P(None, 'feat', 'row'), may hold values from -6 to 6
- inverse_fisher: float32 [16384, 16384], P('row', 'feat'), as said below
- examples: bfloat16 [24576, 16384], P('row', 'feat'), may hold values from -0.046875 to 0.046875
Outputs:
- scores: float32 [2, 768, 24576], P(None, 'feat', 'row')
Inputs may be any that keep to these rules, and one draw needn't show every extreme that they name: `inverse_fisher`: symmetric.
All inputs are finite; a program needn't handle non-finite values.
Results may differ from a plain program's by a relative error of at most 0.0029.
Values may be sent and summed in bfloat16 or wider, within the bound.
A program may use at most 128 MiB of HBM per device.

v0:
```python
import functools
import math

import jax
import jax.numpy as jnp
from jax import lax
from jax.experimental import pallas as pl
from jax.experimental.pallas import tpu as pltpu
from jax.sharding import PartitionSpec as P

F32, BF16 = jnp.float32, jnp.bfloat16
SIZES = (32, 32, 32, 32, 32, 16, 16)
CHUNKS = len(SIZES)
PLACES = tuple(divmod(sum(SIZES[:k]), 96) for k in range(CHUNKS))
BIG = 8 * max(SIZES)
POWER = 9
LIFT = 13
ROOT = 1.0 / (POWER * math.log(2.0))
SLOTS = 4
ACROSS = (5,)
PATTERN = (("A", 0), ("D", 3), ("E", 4), ("C", 2), ("G", 6), ("H", 7), ("B", 0), ("R", 1), ("K", 3))


def scale_of(largest):
    scale = jnp.maximum(largest, 2.0**-90).astype(BF16).astype(F32)
    return scale, (2.0**LIFT) / (scale * 0.0625)


def code(value, factor):
    v = (value * 0.0625) * factor
    v2 = v * v
    v4 = v2 * v2
    return (v4 * v4 * v).astype(BF16)


def decode(coded, scale):
    w = coded.astype(F32)
    size = jnp.exp2(jnp.log(jnp.abs(w)) * ROOT) * (scale * 2.0**-LIFT)
    return jnp.where(w < 0, -size, size)


def fold_max(block):
    rows = block.shape[0]
    return jnp.max(jnp.abs(block).reshape(rows // 8, 8, 128), axis=0)


def kernel(q, f_hbm, e_hbm, out, qh, ql, fst, fh, fl, e, pp, cx, qm, psend, pry, pair, prx, pf, ss, srx, ysend, yrx,
           load_sem, e_sem, q_s, q_r, cx_s, cx_r, h_s, h_r, p_s, p_r, g_s, g_r, k_s, k_r, s_s, s_r, y_s, y_r):
    r, f = lax.axis_index("row"), lax.axis_index("feat")
    x, yl = f % 4, f // 4
    c, chip = r % 2, r // 2
    z, yh = chip % 4, chip // 4
    sibling = (chip * 2 + (1 - c), f)
    ypeer = (r, (1 - yl) * 4 + x)

    def xpeer(d):
        return (r, yl * 4 + (x + d) % 4)

    def chip_at(j):
        return ((yh + j // 4) % 2) * 4 + (z + j % 4) % 4

    def rpeer(j):
        return (chip_at(j) * 2 + c, f)

    def remote(src, dst, send, recv, device):
        return pltpu.make_async_remote_copy(
            src_ref=src, dst_ref=dst, send_sem=send, recv_sem=recv, device_id=device,
            device_id_type=pl.DeviceIdType.MESH)

    def load_f(i, slot):
        return pltpu.make_async_copy(f_hbm.at[pl.ds(i * 128, 128), :], fst.at[slot], load_sem.at[slot])

    for i in range(SLOTS):
        load_f(i, i).start()
    load_e = pltpu.make_async_copy(e_hbm, e, e_sem.at[0])

    peers = [sibling, ypeer] + [xpeer(d) for d in (1, 2, 3)] + [rpeer(j) for j in range(1, 8)]
    barrier = pltpu.get_barrier_semaphore()
    for peer in peers:
        pl.semaphore_signal(barrier, inc=1, device_id=peer, device_id_type=pl.DeviceIdType.MESH)

    def code_queries(k):
        (group, first), own, m = PLACES[k], SIZES[k], 8 * SIZES[k]
        largest = jnp.zeros((8, 128), F32)
        for b in range(8):
            largest = jnp.maximum(largest, fold_max(q[group, first:first + own, b * 128:(b + 1) * 128]))
        scale, factor = scale_of(jnp.max(largest, axis=0, keepdims=True))
        for b in range(8):
            qm[k][0, b * own:(b + 1) * own, :] = code(q[group, first:first + own, b * 128:(b + 1) * 128], factor)
        qm[k][0, m:m + 16, :] = jnp.broadcast_to(scale, (16, 128)).astype(BF16)

    def q_y(k):
        return remote(qm[k].at[0], qm[k].at[4], q_s.at[k, 4], q_r.at[k, 4], ypeer)

    def q_x(k, s, d):
        return remote(qm[k].at[s], qm[k].at[s + d], q_s.at[k, s + d], q_r.at[k, s + d], xpeer(d))

    code_queries(0)
    pl.semaphore_wait(barrier, len(peers))
    for k in range(CHUNKS):
        if k:
            code_queries(k)
        q_y(k).start()
        if k == 0:
            for d in (2, 1, 3):
                q_x(0, 0, d).start()

    def split_f(i):
        slot = i % SLOTS
        load_f(i, slot).wait()
        for half in range(2):
            part = fst[slot, :, half * 1024:(half + 1) * 1024]
            high = part.astype(BF16)
            rows = pl.ds(pl.multiple_of(i * 128, 128), 128)
            fh[half, rows, :] = high
            fl[half, rows, :] = (part - high.astype(F32)).astype(BF16)

        @pl.when(i + SLOTS < 8)
        def _():
            load_f(i + SLOTS, slot).start()

    def forward(k):
        q_y(k).wait_recv()
        for d in (2, 1, 3):
            q_x(k, 4, d).start()
        if k + 1 < CHUNKS:
            for d in (2, 1, 3):
                q_x(k + 1, 0, d).start()

    forward(0)
    forward(1)
    lax.fori_loop(0, 4, lambda i, _: (split_f(i), 0)[1], 0)
    forward(2)
    lax.fori_loop(4, 8, lambda i, _: (split_f(i), 0)[1], 0)
    forward(3)
    load_e.start()

    def cross(k):
        return remote(pp.at[1 - c, 0:8 * SIZES[k]], cx.at[k % 2, 0:8 * SIZES[k]], cx_s.at[k], cx_r.at[k], sibling)

    def stage_a(k):
        own, m = SIZES[k], 8 * SIZES[k]
        if k + 4 < CHUNKS:
            forward(k + 4)
        for j in range(8):
            if j % 4:
                q_x(k, j // 4 * 4, j % 4).wait_recv()
            place = (((x + 4 - j % 4) % 4) * 2 + (yl + j // 4) % 2) * own
            rows = pl.ds(pl.multiple_of(place, 16), own)
            scale = qm[k][j, m:m + 16, :].astype(F32)[0:1]
            for b in range(8):
                value = decode(qm[k][j, b * own:(b + 1) * own, :], scale)
                high = value.astype(BF16)
                qh[rows, b * 128:(b + 1) * 128] = high
                ql[rows, b * 128:(b + 1) * 128] = (value - high.astype(F32)).astype(BF16)
        if k:
            cross(k - 1).wait_send()

        def product(half):
            @pl.loop(0, 2)
            def _(n):
                cols = pl.ds(pl.multiple_of(n * 512, 512), 512)
                total = jnp.dot(qh[0:m, :], fh[half, :, cols], preferred_element_type=F32)
                total += jnp.dot(qh[0:m, :], fl[half, :, cols], preferred_element_type=F32)
                total += jnp.dot(ql[0:m, :], fh[half, :, cols], preferred_element_type=F32)
                pp[half, 0:m, cols] = total

        product(1 - c)
        cross(k).start()
        product(c)

    def h_to(k):
        return remote(psend[k].at[pl.ds((1 - yh) * 4, 4)], pry[k], h_s.at[k], h_r.at[k], rpeer(4))

    def p_to(k, d):
        return remote(pair[k].at[(z + d) % 4], prx[k].at[d - 1], p_s.at[k, d], p_r.at[k, d], rpeer(d))

    def put_coded(m, tiles, ref, b):
        step = m // len(tiles)
        largest = functools.reduce(jnp.maximum, [fold_max(tile) for tile in tiles])
        scale, factor = scale_of(jnp.max(largest, axis=0, keepdims=True))
        for t, tile in enumerate(tiles):
            ref[b, t * step:(t + 1) * step, :] = code(tile, factor)
        ref[b, m:m + 16, :] = jnp.broadcast_to(scale, (16, 128)).astype(BF16)

    def stage_b(k):
        m = 8 * SIZES[k]
        step = m // 4
        cross(k).wait_recv()

        @pl.loop(0, 8)
        def _(b):
            cols = pl.ds(pl.multiple_of(b * 128, 128), 128)
            put_coded(m, [pp[c, t:t + step, cols] + cx[k % 2, t:t + step, cols] for t in range(0, m, step)], psend[k], b)

        h_to(k).start()

    def stage_r(k):
        m = 8 * SIZES[k]
        step = m // 4
        h_to(k).wait_recv()

        @pl.loop(0, 4)
        def _(b):
            mine_scale = psend[k][yh * 4 + b, m:m + 16, :].astype(F32)[0:1]
            scale = pry[k][b, m:m + 16, :].astype(F32)[0:1]
            put_coded(m, [decode(psend[k][yh * 4 + b, t:t + step, :], mine_scale) + decode(pry[k][b, t:t + step, :], scale)
                          for t in range(0, m, step)], pair[k], b)

        for d in (2, 1, 3):
            p_to(k, d).start()

    mine = c * 8 + chip

    def g_y(k):
        return remote(pf[k].at[mine], pf[k].at[mine], g_s.at[k, 4], g_r.at[k, 4], rpeer(4))

    def g_z(k, s, d):
        piece = c * 8 + chip_at(s)
        return remote(pf[k].at[piece], pf[k].at[piece], g_s.at[k, s + d], g_r.at[k, s + d], rpeer(d))

    def stage_c(k):
        m, step = 8 * SIZES[k], SIZES[k]
        for d in (1, 2, 3):
            p_to(k, d).wait_recv()
        scales = [pair[k][z, m:m + 16, :].astype(F32)[0:1]]
        scales += [prx[k][d, m:m + 16, :].astype(F32)[0:1] for d in range(3)]

        @pl.loop(0, 8)
        def _(t):
            rows = pl.ds(pl.multiple_of(t * step, 16), step)
            total = decode(pair[k][z, rows, :], scales[0])
            for d in range(3):
                total += decode(prx[k][d, rows, :], scales[d + 1])
            pf[k][mine, rows, :] = total.astype(BF16)

        g_y(k).start()
        for d in (1, 3, 2):
            g_z(k, 0, d).start()

    def stage_d(k):
        g_y(k).wait_recv()
        for d in (1, 3, 2):
            g_z(k, 4, d).start()

    def whole(k):
        return remote(pf[k].at[pl.ds(c * 8, 8)], pf[k].at[pl.ds(c * 8, 8)], k_s.at[k], k_r.at[k], sibling)

    def stage_k(k):
        for s in (0, 4):
            for d in (1, 3, 2):
                g_z(k, s, d).wait_recv()
        whole(k).start()

    def s_to(k, d):
        if k in ACROSS:
            src, dst = ysend[k].at[(x + d) % 4], srx[k].at[d - 1, 0:SIZES[k]]
        else:
            src, dst = ss[k].at[(x + d) % 4], srx[k].at[d - 1]
        return remote(src, dst, s_s.at[k, d - 1], s_r.at[k, d - 1], xpeer(d))

    def y_to(k):
        own = SIZES[k]
        if k in ACROSS:
            src = ss[k].at[:, pl.ds(pl.multiple_of((1 - yl) * own, 16), own), :]
        else:
            src = ysend[k]
        return remote(src, yrx[k], y_s.at[k], y_r.at[k], ypeer)

    def stage_e(k):
        if k == 0:
            load_e.wait()
        whole(k).wait_recv()

        @pl.loop(0, 3)
        def _(n):
            rows = pl.ds(pl.multiple_of(n * 512, 512), 512)
            left = jnp.concatenate([pf[k][g] for g in range(16)], axis=1)
            total = lax.dot_general(left, e[rows, :], (((1,), (1,)), ((), ())), preferred_element_type=F32)
            ss[k][:, :, rows] = total.astype(BF16).reshape(4, 2 * SIZES[k], 512)

        if k in ACROSS:
            y_to(k).start()
        else:
            for d in (1, 3, 2):
                s_to(k, d).start()

    def across(k):
        (group, first), own = PLACES[k], SIZES[k]
        y_to(k).wait_recv()

        def summed(b, t, cols):
            rows = pl.ds(pl.multiple_of(yl * own + t, 16), 16)
            return ss[k][b, rows, cols].astype(F32) + yrx[k][b, t:t + 16, cols].astype(F32)

        @pl.loop(0, 3)
        def _(n):
            cols = pl.ds(pl.multiple_of(n * 512, 512), 512)
            for t in range(0, own, 16):
                for b in range(4):
                    ysend[k][b, t:t + 16, cols] = summed(b, t, cols).astype(BF16)

        for d in (1, 3, 2):
            s_to(k, d).start()

        @pl.loop(0, 3)
        def _(n):
            cols = pl.ds(pl.multiple_of(n * 512, 512), 512)
            for t in range(0, own, 16):
                out[group, first + t:first + t + 16, cols] = summed(x, t, cols)

    def stage_g(k):
        if k in ACROSS:
            across(k)
            return
        (group, first), own = PLACES[k], SIZES[k]
        for d in (1, 2, 3):
            s_to(k, d).wait_recv()

        def summed(part, rows, cols):
            rows = pl.ds(pl.multiple_of(part * own + rows, 16), 16)
            total = ss[k][x, rows, cols].astype(F32)
            for d in range(3):
                total += srx[k][d, rows, cols].astype(F32)
            return total

        @pl.loop(0, 3)
        def _(n):
            cols = pl.ds(pl.multiple_of(n * 512, 512), 512)
            for t in range(0, own, 16):
                ysend[k][t:t + 16, cols] = summed(1 - yl, t, cols).astype(BF16)

        y_to(k).start()

        @pl.loop(0, 3)
        def _(n):
            cols = pl.ds(pl.multiple_of(n * 512, 512), 512)
            for t in range(0, own, 16):
                out[group, first + t:first + t + 16, cols] = summed(yl, t, cols)

    def stage_h(k):
        (group, first), own = PLACES[k], SIZES[k]
        if k in ACROSS:
            for d in (1, 2, 3):
                s_to(k, d).wait_recv()
        else:
            y_to(k).wait_recv()

        @pl.loop(0, 3)
        def _(n):
            cols = pl.ds(pl.multiple_of(n * 512, 512), 512)
            if k in ACROSS:
                for t in range(0, own, 16):
                    rows = slice(first + t, first + t + 16)
                    out[group, rows, cols] += sum(srx[k][d, t:t + 16, cols].astype(F32) for d in range(3))
                return
            out[group, first:first + own, cols] += yrx[k][:, cols].astype(F32)

    stages = dict(A=stage_a, B=stage_b, R=stage_r, C=stage_c, D=stage_d, K=stage_k, E=stage_e, G=stage_g, H=stage_h)
    for turn in range(CHUNKS + max(late for _, late in PATTERN)):
        for name, late in PATTERN:
            if 0 <= turn - late < CHUNKS:
                stages[name](turn - late)

    for k in range(CHUNKS):
        q_y(k).wait_send()
        for s in (0, 4):
            for d in (1, 2, 3):
                q_x(k, s, d).wait_send()
                g_z(k, s, d).wait_send()
        h_to(k).wait_send()
        for d in (1, 2, 3):
            p_to(k, d).wait_send()
        g_y(k).wait_send()
        whole(k).wait_send()
        for d in (1, 2, 3):
            s_to(k, d).wait_send()
        y_to(k).wait_send()
    cross(CHUNKS - 1).wait_send()


def body(queries, inverse_fisher, examples):
    dma = pltpu.SemaphoreType.DMA
    n = CHUNKS

    def each(shape):
        return [pltpu.VMEM(shape(o), BF16) for o in SIZES]

    return pl.pallas_call(
        kernel,
        out_shape=jax.ShapeDtypeStruct((2, 96, 1536), F32),
        in_specs=[pl.BlockSpec(memory_space=pltpu.VMEM), pl.BlockSpec(memory_space=pl.ANY),
                  pl.BlockSpec(memory_space=pl.ANY)],
        out_specs=pl.BlockSpec(memory_space=pltpu.VMEM),
        scratch_shapes=[
            pltpu.VMEM((BIG, 1024), BF16),
            pltpu.VMEM((BIG, 1024), BF16),
            pltpu.VMEM((SLOTS, 128, 2048), F32),
            pltpu.VMEM((2, 1024, 1024), BF16),
            pltpu.VMEM((2, 1024, 1024), BF16),
            pltpu.VMEM((1536, 2048), BF16),
            pltpu.VMEM((2, BIG, 1024), F32),
            pltpu.VMEM((2, BIG, 1024), F32),
            each(lambda o: (8, 8 * o + 16, 128)),
            each(lambda o: (8, 8 * o + 16, 128)),
            each(lambda o: (4, 8 * o + 16, 128)),
            each(lambda o: (4, 8 * o + 16, 128)),
            each(lambda o: (3, 8 * o + 16, 128)),
            each(lambda o: (16, 8 * o, 128)),
            each(lambda o: (4, 2 * o, 1536)),
            each(lambda o: (3, 2 * o, 1536)),
            [pltpu.VMEM((4, o, 1536) if k in ACROSS else (o, 1536), BF16) for k, o in enumerate(SIZES)],
            [pltpu.VMEM((4, o, 1536) if k in ACROSS else (o, 1536), BF16) for k, o in enumerate(SIZES)],
            dma((SLOTS,)), dma((1,)),
            dma((n, 8)), dma((n, 8)),
            dma((n,)), dma((n,)),
            dma((n,)), dma((n,)),
            dma((n, 4)), dma((n, 4)),
            dma((n, 8)), dma((n, 8)),
            dma((n,)), dma((n,)),
            dma((n, 3)), dma((n, 3)),
            dma((n,)), dma((n,)),
        ],
        compiler_params=pltpu.CompilerParams(
            collective_id=0, has_side_effects=True, vmem_limit_bytes=60 * 2**20),
        cost_estimate=pl.CostEstimate(flops=29_000_000_000, bytes_accessed=17_000_000, transcendentals=0),
        name="influence",
    )(queries, inverse_fisher, examples)


def solution(mesh):
    return jax.shard_map(
        body,
        mesh=mesh,
        in_specs=(P(None, "feat", "row"), P("row", "feat"), P("row", "feat")),
        out_specs=P(None, "feat", "row"),
        check_vma=False,
    )
```

profile of v0, /device:TPU:1, one launch (start us, length us, event | category | flops | bytes accessed | tf_op | source)
XLA Modules:
  0.0 119.5 jit_solution(17711468305779332302)
XLA Ops:
  0.0 117.1 %influence.1 = f32[2,96,1536]{2,1,0:T(8,128)} custom-call(f32[2,96,1024]{2,1,0:T(8,128)} %q.1, f32[1024,2048]{1,0:T(8,128)} %f_hbm.1, bf16[1536,2048]{1,0:T(8,128)(2,1)} %e_hbm.1), custom_call_target="tpu_custom_call" | custom-call | flops 28999999488 | bytes 17000000 | tf_op jit(solution)/shard_map/influence/pallas_call | solution.py:389
  117.1 2.4 %copy.5 = f32[2,96,1536]{2,1,0:T(8,128)} copy(f32[2,96,1536]{2,1,0:T(8,128)} %influence.1) | data formatting | bytes 2359296
where the time goes:
time: 120 us; the launch traced here: 119 us
  Pallas kernels  117 us (98%)
  local copies, waits for them, and re-layouts  2.36 us (2%)
    pallas_call x1, Pallas kernels, body(): pl.pallas_call(kernel, out_shape=jax.ShapeDtypeStruct((2, 96, 1536), F32)...  117 us

commit v1 on v0

--- a/solution.py
+++ b/solution.py
@@ -252,12 +252,13 @@
                 g_z(k, s, d).wait_recv()
         whole(k).start()
 
-    def s_to(k, d):
+    def s_to(k, d, n=0):
+        cols = slice(n * 512, (n + 1) * 512)
         if k in ACROSS:
             src, dst = ysend[k].at[(x + d) % 4], srx[k].at[d - 1, 0:SIZES[k]]
         else:
-            src, dst = ss[k].at[(x + d) % 4], srx[k].at[d - 1]
-        return remote(src, dst, s_s.at[k, d - 1], s_r.at[k, d - 1], xpeer(d))
+            src, dst = ss[k].at[(x + d) % 4, :, cols], srx[k].at[d - 1, :, cols]
+        return remote(src, dst, s_s.at[k, n, d - 1], s_r.at[k, n, d - 1], xpeer(d))
 
     def y_to(k):
         own = SIZES[k]
@@ -272,18 +273,17 @@
             load_e.wait()
         whole(k).wait_recv()
 
-        @pl.loop(0, 3)
-        def _(n):
-            rows = pl.ds(pl.multiple_of(n * 512, 512), 512)
+        for n in range(3):
+            rows = slice(n * 512, (n + 1) * 512)
             left = jnp.concatenate([pf[k][g] for g in range(16)], axis=1)
             total = lax.dot_general(left, e[rows, :], (((1,), (1,)), ((), ())), preferred_element_type=F32)
             ss[k][:, :, rows] = total.astype(BF16).reshape(4, 2 * SIZES[k], 512)
+            if k not in ACROSS:
+                for d in (2, 1, 3):
+                    s_to(k, d, n).start()
 
         if k in ACROSS:
             y_to(k).start()
-        else:
-            for d in (1, 3, 2):
-                s_to(k, d).start()
 
     def across(k):
         (group, first), own = PLACES[k], SIZES[k]
@@ -314,8 +314,9 @@
             across(k)
             return
         (group, first), own = PLACES[k], SIZES[k]
-        for d in (1, 2, 3):
-            s_to(k, d).wait_recv()
+        for n in range(3):
+            for d in (1, 2, 3):
+                s_to(k, d, n).wait_recv()
 
         def summed(part, rows, cols):
             rows = pl.ds(pl.multiple_of(part * own + rows, 16), 16)
@@ -373,8 +374,9 @@
             p_to(k, d).wait_send()
         g_y(k).wait_send()
         whole(k).wait_send()
-        for d in (1, 2, 3):
-            s_to(k, d).wait_send()
+        for n in range(1 if k in ACROSS else 3):
+            for d in (1, 2, 3):
+                s_to(k, d, n).wait_send()
         y_to(k).wait_send()
     cross(CHUNKS - 1).wait_send()
 
@@ -418,7 +420,7 @@
             dma((n, 4)), dma((n, 4)),
             dma((n, 8)), dma((n, 8)),
             dma((n,)), dma((n,)),
-            dma((n, 3)), dma((n, 3)),
+            dma((n, 3, 3)), dma((n, 3, 3)),
             dma((n,)), dma((n,)),
         ],
         compiler_params=pltpu.CompilerParams(

time: 120 us -> 119 us (level)
  no operation moved by 1% of the time
where the time goes in v1:
time: 119 us; the launch traced here: 118 us
  Pallas kernels  116 us (97%)
  local copies, waits for them, and re-layouts  2.36 us (2%)
    pallas_call x1, Pallas kernels, body(): pl.pallas_call(kernel, out_shape=jax.ShapeDtypeStruct((2, 96, 1536), F32)...  116 us

profile of v1, /device:TPU:1, one launch (start us, length us, event | category | flops | bytes accessed | tf_op | source)
XLA Modules:
  0.0 118.4 jit_solution(3046816830585741738)
XLA Ops:
  0.0 116.1 %influence.1 = f32[2,96,1536]{2,1,0:T(8,128)} custom-call(f32[2,96,1024]{2,1,0:T(8,128)} %q.1, f32[1024,2048]{1,0:T(8,128)} %f_hbm.1, bf16[1536,2048]{1,0:T(8,128)(2,1)} %e_hbm.1), custom_call_target="tpu_custom_call" | custom-call | flops 28999999488 | bytes 17000000 | tf_op jit(solution)/shard_map/influence/pallas_call | solution.py:391
  116.1 2.4 %copy.5 = f32[2,96,1536]{2,1,0:T(8,128)} copy(f32[2,96,1536]{2,1,0:T(8,128)} %influence.1) | data formatting | bytes 2359296
